TPU v7x, 32 devices: a whole 2x2x4 slice. The times are simulated.
32 devices in a mesh: seg: 8 (over z, y), blk: 4 (over x, core).
Axes of the slice: x: 2, y: 2, z: 4, core: 2. Of those that a mesh axis runs over, the one named last changes fastest.
Arguments:
- queries: float32 [4096, 1024], P(('seg', 'blk')), may hold values from -5 to 5
- keys: float32 [4096, 256], P(('seg', 'blk')), may hold values from -5 to 5
- values: float32 [4096, 256], P(('seg', 'blk')), may hold values from -6 to 6
- gate_logit: float32 [8], replicated, may hold values from -3 to 3
- memory_gain: float32 [1024], replicated, may hold values from 0.5 to 2
Outputs:
- mixed: float32 [4096, 1024], P(('seg', 'blk'))
All inputs are finite; a program needn't handle non-finite values.
Results may differ from a plain program's by a relative error of at most 0.0003.
Values sent between devices are 32-bit elements; how exact they have to be, the bound alone decides.
No kernel may reach another device: no remote copies, remote signals or barrier semaphores. Data moves between devices by JAX's collectives and lax.ppermute only.
A program may use at most 64 MiB of HBM per device.

v0:
```python
import jax
import jax.numpy as jnp
from jax import lax
from jax.sharding import PartitionSpec as P

QH = 8
KVH = 2
GROUP = 4
HD = 128
HIGH = lax.Precision.HIGHEST


def prefix_2(part, axis, combine, identity):
    place = lax.axis_index(axis)
    gathered = lax.all_gather(part, axis)
    state = jnp.zeros_like(part) + jnp.asarray(identity, part.dtype)

    def one(lap, state):
        return combine(state, lax.dynamic_index_in_dim(gathered, lap, 0, False))

    return lax.fori_loop(0, place, one, state)


def sigma_map(x):
    return jnp.where(x > 0, x + 1.0, jnp.exp(jnp.minimum(x, 0.0)))


def add_terms(earlier, later):
    return earlier + later


def on_device(queries, keys, values, gate_logit, memory_gain):
    rows = queries.shape[0]
    index = lax.axis_index("blk")
    q_heads = queries.reshape(rows, KVH, GROUP, HD)
    qpos = index * rows + jnp.arange(rows, dtype=jnp.int32)
    scale = 1.0 / jnp.sqrt(jnp.float32(HD))

    def update(carry, pieces):
        top, total, accum = carry
        k_piece, v_piece = pieces
        count = k_piece.shape[0]
        k_h = k_piece.reshape(count, KVH, HD)
        v_h = v_piece.reshape(count, KVH, HD)
        scores = jnp.einsum("rkgd,nkd->kgrn", q_heads, k_h, precision=HIGH) * scale
        kpos = jnp.arange(count, dtype=jnp.int32)
        allowed = (kpos[None, :] <= qpos[:, None])[None, None]
        row_top = jnp.max(jnp.where(allowed, scores, -1e30), axis=-1)
        new_top = jnp.maximum(top, row_top)
        weights = jnp.where(allowed, jnp.exp(scores - new_top[..., None]), 0.0)
        total = jnp.sum(weights, axis=-1)
        accum = jnp.einsum("kgrn,nkd->kgrd", weights, v_h, precision=HIGH)
        return (new_top, total, accum)

    start_state = (
        jnp.full((KVH, GROUP, rows), -1e30, jnp.float32),
        jnp.zeros((KVH, GROUP, rows), jnp.float32),
        jnp.zeros((KVH, GROUP, rows, HD), jnp.float32),
    )
    pieces = (
        lax.all_gather(keys, "blk", axis=0, tiled=True),
        lax.all_gather(values, "blk", axis=0, tiled=True),
    )
    top, total, accum = lax.cond(
        jnp.int32(0) <= qpos[rows - 1], lambda c: update(c, pieces), lambda c: c, start_state
    )
    attention = accum / total[..., None]
    sig_keys = sigma_map(keys.reshape(rows, KVH, HD))
    partial_value = jnp.einsum(
        "rkd,rke->kde", sig_keys, values.reshape(rows, KVH, HD), precision=HIGH
    ).reshape(KVH * HD, HD)
    shard = lax.psum_scatter(partial_value, "blk", scatter_dimension=0, tiled=True)
    prefix = prefix_2(shard, "seg", add_terms, jnp.zeros_like(shard))
    memory = lax.all_gather(prefix, "blk", axis=0, tiled=True)
    retrieval = jnp.einsum(
        "rkgd,kde->kgre", sigma_map(q_heads), memory.reshape(KVH, HD, HD), precision=HIGH
    )
    rms = jnp.sqrt(jnp.mean(retrieval * retrieval, axis=-1, keepdims=True) + 1e-06)
    normed = retrieval / rms * memory_gain.reshape(KVH, GROUP, 1, HD)
    gate = jax.nn.sigmoid(gate_logit).reshape(KVH, GROUP, 1, 1)
    mixed = gate * normed + (1.0 - gate) * attention
    return jnp.transpose(mixed, (2, 0, 1, 3)).reshape(rows, QH * HD)


def solution(mesh):
    return jax.shard_map(
        on_device,
        mesh=mesh,
        in_specs=(
            P(("seg", "blk"), None),
            P(("seg", "blk"), None),
            P(("seg", "blk"), None),
            P(),
            P(),
        ),
        out_specs=P(("seg", "blk"), None),
        check_vma=False,
    )
```

profile of v0, /device:TPU:0, one launch (start us, length us, event | category | flops | bytes accessed | tf_op | source)
XLA Modules:
  0.0 82.2 jit_solution(3702383600021202158)
XLA Ops:
  6.5 0.0 reduce-scatter.2.cloned.1.call-start
  6.5 1.0 %exponential_select_fusion = f32[128,256]{1,0:T(8,128)S(1)} fusion(f32[128,256]{1,0:T(8,128)} %param.10), kind=kLoop, calls=%fused_computation.32 | loop fusion | flops 131072 | bytes 262144 | tf_op jit(solution)/shard_map/jit(_where)/select_n | solution.py:25
  7.5 0.1 copy.34
  7.6 1.8 %fusion.22 = f32[2,128,128]{2,1,0:T(8,128)} fusion(f32[128,2,128]{0,2,1:T(8,128)S(1)} %bitcast.51, f32[128,256]{1,0:T(8,128)} %param.11), kind=kOutput, calls=%fused_computation.29 | convolution fusion | flops 50331648 | bytes 393216 | tf_op jit(solution)/shard_map/rkd,rke->kde/dot_general | solution.py:69
  9.5 0.0 reduce-scatter.2.cloned.1.call-update
  9.5 8.8 %all_gather.18 = f32[512,256]{1,0:T(8,128)S(1)} all-gather(f32[128,256]{1,0:T(8,128)} %param.10), channel_id=1, replica_groups=mesh['seg'=8,'blk'=4] {'blk'}, dimensions={0}, use_global_device_ids=true | all-gather | bytes 655360 | tf_op jit(solution)/shard_map/all_gather | solution.py:61
  18.3 8.8 %all_gather.19 = f32[512,256]{1,0:T(8,128)} all-gather(f32[128,256]{1,0:T(8,128)} %param.11), channel_id=1, replica_groups=mesh['seg'=8,'blk'=4] {'blk'}, dimensions={0}, use_global_device_ids=true | all-gather | bytes 655360 | tf_op jit(solution)/shard_map/all_gather | solution.py:62
  27.2 0.0 copy-done.2
  27.2 0.2 copy.18
  27.4 0.6 slice.3
  28.6 0.1 mul.40
  28.7 6.7 %conditional.1 = (f32[2,4,128]{2,1,0:T(4,128)S(1)}, f32[2,4,128,128]{2,3,1,0:T(8,128)}) conditional(s32[]{:T(128)} %bitcast.12, () %tuple.18, (s32[128]{0:T(128)S(1)}, f32[512,256]{1,0:T(8,128)S(1)}, f32[128,2,4,128]{0,3,2,1:T(8,128)S(1)}, f32[512,256]{1,0:T(8,128)}) %tuple.40), branch_computations={%region_4.5_spmd, %region_5.8_spmd} | conditional | flops 1615920128 | bytes 10773008 | solution.py:64
  28.8 0.3 reshape.68
  29.0 2.0 %fusion = (f32[2,4,128]{2,1,0:T(4,128)S(1)}, f32[2,512,128,4]{2,1,3,0:T(8,128)S(1)}) fusion(pred[128,512]{0,1:T(8,128)(4,1)S(1)} %iota_compare_fusion, f32[128,2,4,128]{0,3,2,1:T(8,128)S(1)} %get-tuple-element.47, f32[512,2,128,1]{2,1,0,3:T(2,128)S(1)} %bitcast.46), kind=kOutput, calls=%fused_computation.3 | convolution fusion | flops 806878208 | bytes 3215360 | tf_op jit(solution)/shard_map/cond/branch_1_fun/rkgd,nkd->kgrn/dot_general | solution.py:45
  31.0 1.3 %reshape.69 = f32[512,2,128]{2,1,0:T(2,128)S(1)} reshape(f32[512,256]{1,0:T(8,128)} %get-tuple-element.38) | data formatting | bytes 1048576 | tf_op jit(solution)/shard_map/cond/branch_1_fun/reshape | solution.py:44
  32.3 2.6 %fusion.3 = f32[2,4,128,128]{2,3,1,0:T(8,128)} fusion(f32[2,512,128,4]{2,1,3,0:T(8,128)S(1)} %get-tuple-element.59, f32[2,4,128]{2,1,0:T(4,128)S(1)} %broadcast_maximum_fusion, pred[128,512]{0,1:T(8,128)(4,1)S(1)} %iota_compare_fusion, f32[512,2,128,1]{2,1,0,3:T(2,128)S(1)} %bitcast.52), kind=kOutput, calls=%fused_computation.6 | convolution fusion | flops 806879232 | bytes 3215360 | tf_op jit(solution)/shard_map/cond | solution.py:64
  34.9 0.4 fusion.5
  35.4 0.0 copy-start.1
  35.4 0.0 reduce-scatter.2.cloned.1.call-done
  35.4 31.5 %all-gather = f32[512,128]{1,0:T(8,128)S(1)} all-gather(f32[64,128]{1,0:T(8,128)} %reduce-scatter.2.cloned.1.call-done), channel_id=2, replica_groups=mesh['seg'=8,'blk'=4] {'seg'}, dimensions={0}, use_global_device_ids=true | all-gather | bytes 294912 | tf_op jit(solution)/shard_map/all_gather | solution.py:15
  66.9 5.4 %all_gather.17 = f32[256,128]{1,0:T(8,128)S(1)} all-gather(f32[64,128]{1,0:T(8,128)S(1)} %get-tuple-element.42), channel_id=1, replica_groups=mesh['seg'=8,'blk'=4] {'blk'}, dimensions={0}, use_global_device_ids=true | all-gather | bytes 163840 | tf_op jit(solution)/shard_map/all_gather | solution.py:74
  72.3 0.7 multiply_reduce_fusion
  73.0 1.3 %multiply_add_fusion = f32[2,4,128,128]{2,3,1,0:T(8,128)S(1)} fusion(f32[2,4,128,128]{2,3,1,0:T(8,128)} %get-tuple-element.49, f32[2,4,128,128]{2,3,1,0:T(8,128)S(1)} %get-tuple-element.61, f32[2,4,128]{2,1,0:T(4,128)S(1)} %get-tuple-element.44, f32[2,4]{1,0:T(2,128)S(1)} %broadcast_subtract_fusion, f32[2,4,128]{2,1,0:T(4,128)S(1)} %bitcast.53, ...), kind=kLoop, calls=%fused_computation.20 | loop fusion | flops 786432 | bytes 1585216 | tf_op jit(solution)/shard_map/add | solution.py:81
  74.3 1.0 %copy.23 = f32[128,1024]{1,0:T(8,128)} copy(f32[128,1024]{0,1:T(8,128)S(1)} %bitcast.47) | data formatting | bytes 1048576 | tf_op jit(solution)/shard_map/reshape | solution.py:82
  (12 shorter events, 0.1 us)
Async XLA Ops:
  6.5 20.6 %copy-start.2 = (f32[8]{0:T(128)S(1)}, f32[8]{0:T(128)}, u32[]{:S(2)}) copy-start(f32[8]{0:T(128)} %param.12) | copy-start | bytes 100
  6.5 20.6 %copy-start = (f32[128,1024]{1,0:T(8,128)S(1)}, f32[128,1024]{1,0:T(8,128)}, u32[]{:S(2)}) copy-start(f32[128,1024]{1,0:T(8,128)} %param.9) | copy-start | bytes 1572868
  6.5 28.9 %reduce-scatter.2.cloned.1.call-start = ((), (), s32[]{:S(2)}) async-start(), calls=%async_computation.1 | async-start | bytes 163840 | tf_op jit(solution)/shard_map/reduce_scatter | solution.py:72
  35.4 37.7 %copy-start.1 = (f32[1024]{0:T(1024)S(1)}, f32[1024]{0:T(1024)}, u32[]{:S(2)}) copy-start(f32[1024]{0:T(1024)} %param.13) | copy-start | bytes 12292
Sparse Core Ops, SparseCore 0:
  9.8 22.2 reduce-scatter.1
where the time goes:
time: 82.5 us; the launch traced here: 82.2 us
  blocking collectives  54.6 us (66%)
  between operations  14.1 us (17%)
  matrix products  7.09 us (9%)
  local copies, waits for them, and re-layouts  3.53 us (4%)
  other arithmetic  2.79 us (3%)
    all_gather x1, blocking collectives, prefix_2(): gathered = lax.all_gather(part, axis)  31.5 us
    all_gather x1, blocking collectives, on_device(): lax.all_gather(values, 'blk', axis=0, tiled=True)  8.84 us
    all_gather x1, blocking collectives, on_device(): lax.all_gather(keys, 'blk', axis=0, tiled=True)  8.83 us
    all_gather x1, blocking collectives, on_device(): memory = lax.all_gather(prefix, 'blk', axis=0, tiled=True)  5.42 us
    cond x1, matrix products, on_device(): lax.cond(jnp.int32(0) <= qpos[rows - 1], lambda c: update(c, pieces), lam...  2.61 us
    dot_general x1, matrix products, update(): scores = jnp.einsum('rkgd,nkd->kgrn', q_heads, k_h, precision=HIGH) * scale  1.96 us
    dot_general x1, matrix products, on_device(): jnp.einsum('rkd,rke->kde', sig_keys, values.reshape(rows, KVH, HD), preci...  1.83 us
  transfers between devices with their start and end apart: 1, of which 0 were waited for; matrix products, arithmetic and copies ran while one was open for 9% of the time, Pallas kernels for 0%

commit v1 on v0

--- a/solution.py
+++ b/solution.py
@@ -71,7 +71,14 @@
     ).reshape(KVH * HD, HD)
     shard = lax.psum_scatter(partial_value, "blk", scatter_dimension=0, tiled=True)
     prefix = prefix_2(shard, "seg", add_terms, jnp.zeros_like(shard))
-    memory = lax.all_gather(prefix, "blk", axis=0, tiled=True)
+    size = lax.axis_size("blk")
+    right = [(i, (i + 1) % size) for i in range(size)]
+    blocks = [prefix]
+    for reach in range(1, size):
+        blocks = [lax.ppermute(blocks[0], "blk", right), *blocks]
+    result = jnp.concatenate(blocks, axis=0)
+    offset = (lax.axis_index("blk") + 1) * blocks[-1].shape[0]
+    memory = jnp.roll(result, offset, axis=0)
     retrieval = jnp.einsum(
         "rkgd,kde->kgre", sigma_map(q_heads), memory.reshape(KVH, HD, HD), precision=HIGH
     )

time: 82.5 us -> 99.1 us (1.20)
  waiting for transfers between devices: 0.04 us -> 21.9 us
  blocking collectives: 54.6 us -> 46.3 us
  matrix products: 7.09 us -> 8.13 us
    reduce_scatter x1, waiting for transfers between devices: 0.02 us -> 21.8 us  [on_device(): lax.psum_scatter(partial_value, 'blk', scatter_dimension=0, tiled=True)]
    all_gather x1 -> x0, blocking collectives: 5.42 us -> none  [on_device(): memory = lax.all_gather(prefix, 'blk', axis=0, tiled=True)]
    all_gather x1, blocking collectives: 8.83 us -> 7.59 us  [on_device(): lax.all_gather(keys, 'blk', axis=0, tiled=True)]
    all_gather x1, blocking collectives: 8.84 us -> 7.75 us  [on_device(): lax.all_gather(values, 'blk', axis=0, tiled=True)]
    cond x1, matrix products: 2.61 us -> 3.64 us  [on_device(): lax.cond(jnp.int32(0) <= qpos[rows - 1], lambda c: update(c, pieces), lam...]
  transfers between devices with their start and end apart: 1 -> 4, of which waited for: 0 -> 1; matrix products, arithmetic and copies ran while one was open for 9% -> 9% of each run, Pallas kernels for 0% -> 0%
where the time goes in v1:
time: 99.1 us; the launch traced here: 98.7 us
  blocking collectives  46.3 us (47%)
  waiting for transfers between devices  21.9 us (22%)
  between operations  14.2 us (14%)
  matrix products  8.13 us (8%)
  local copies, waits for them, and re-layouts  3.92 us (4%)
  other arithmetic  3.46 us (3%)
    all_gather x1, blocking collectives, prefix_2(): gathered = lax.all_gather(part, axis)  31 us
    reduce_scatter x1, waiting for transfers between devices, on_device(): lax.psum_scatter(partial_value, 'blk', scatter_dimension=0, tiled=True)  21.8 us
    all_gather x1, blocking collectives, on_device(): lax.all_gather(values, 'blk', axis=0, tiled=True)  7.75 us
    all_gather x1, blocking collectives, on_device(): lax.all_gather(keys, 'blk', axis=0, tiled=True)  7.59 us
    cond x1, matrix products, on_device(): lax.cond(jnp.int32(0) <= qpos[rows - 1], lambda c: update(c, pieces), lam...  3.64 us
  transfers between devices with their start and end apart: 4, of which 1 were waited for; matrix products, arithmetic and copies ran while one was open for 9% of the time, Pallas kernels for 0%

profile of v1, /device:TPU:0, one launch (start us, length us, event | category | flops | bytes accessed | tf_op | source)
XLA Modules:
  0.0 98.7 jit_solution(5421183968647977960)
XLA Ops:
  6.5 1.0 %exponential_select_fusion = f32[128,256]{1,0:T(8,128)S(1)} fusion(f32[128,256]{1,0:T(8,128)} %param.10), kind=kLoop, calls=%fused_computation.32 | loop fusion | flops 131072 | bytes 262144 | tf_op jit(solution)/shard_map/jit(_where)/select_n | solution.py:25
  7.6 0.1 copy.34
  7.7 1.8 %fusion.22 = f32[2,128,128]{2,1,0:T(8,128)} fusion(f32[128,2,128]{0,2,1:T(8,128)S(1)} %bitcast.51, f32[128,256]{1,0:T(8,128)} %param.11), kind=kOutput, calls=%fused_computation.29 | convolution fusion | flops 50331648 | bytes 393216 | tf_op jit(solution)/shard_map/rkd,rke->kde/dot_general | solution.py:69
  9.5 0.7 add_divide_fusion
  10.2 0.1 mul.43
  10.3 21.8 %reduce-scatter.2.cloned.1.call-done = f32[64,128]{1,0:T(8,128)} async-done(((f32[256,128]{1,0:T(8,128)}), f32[64,128]{1,0:T(8,128)}) %reduce-scatter.2.cloned.1.call-update) | async-done | bytes 32784 | tf_op jit(solution)/shard_map/reduce_scatter | solution.py:72
  32.1 31.0 %all-gather = f32[512,128]{1,0:T(8,128)S(1)} all-gather(f32[64,128]{1,0:T(8,128)} %reduce-scatter.2.cloned.1.call-done), channel_id=2, replica_groups=mesh['seg'=8,'blk'=4] {'seg'}, dimensions={0}, use_global_device_ids=true | all-gather | bytes 294912 | tf_op jit(solution)/shard_map/all_gather | solution.py:15
  63.1 0.0 collective-permute-start
  63.2 7.6 %all_gather.14 = f32[512,256]{1,0:T(8,128)S(1)} all-gather(f32[128,256]{1,0:T(8,128)S(1)} %copy-done.2), channel_id=1, replica_groups=mesh['seg'=8,'blk'=4] {'blk'}, dimensions={0}, use_global_device_ids=true | all-gather | bytes 655360 | tf_op jit(solution)/shard_map/all_gather | solution.py:61
  70.8 0.3 collective-permute-start.1
  71.1 7.7 %all_gather.15 = f32[512,256]{1,0:T(8,128)} all-gather(f32[128,256]{1,0:T(8,128)S(1)} %copy-done.1), channel_id=1, replica_groups=mesh['seg'=8,'blk'=4] {'blk'}, dimensions={0}, use_global_device_ids=true | all-gather | bytes 655360 | tf_op jit(solution)/shard_map/all_gather | solution.py:62
  78.9 0.3 collective-permute-start.2
  79.2 0.6 slice.3
  80.5 0.2 copy.18
  80.7 8.1 %conditional.1 = (f32[2,4,128]{2,1,0:T(4,128)S(1)}, f32[2,4,128,128]{2,3,1,0:T(8,128)}) conditional(s32[]{:T(128)} %bitcast.12, () %tuple.18, (s32[128]{0:T(128)S(1)}, f32[512,256]{1,0:T(8,128)S(1)}, f32[128,2,4,128]{0,3,2,1:T(8,128)S(1)}, f32[512,256]{1,0:T(8,128)}) %tuple.40), branch_computations={%region_4.5_spmd, %region_5.8_spmd} | conditional | flops 1615920128 | bytes 12870188 | solution.py:64
  80.8 0.3 reshape.68
  81.0 2.0 %fusion = (f32[2,4,128]{2,1,0:T(4,128)S(1)}, f32[2,512,128,4]{2,1,3,0:T(8,128)S(1)}) fusion(pred[128,512]{0,1:T(8,128)(4,1)S(1)} %iota_compare_fusion, f32[128,2,4,128]{0,3,2,1:T(8,128)S(1)} %get-tuple-element.47, f32[512,2,128,1]{2,1,0,3:T(2,128)S(1)} %bitcast.46), kind=kOutput, calls=%fused_computation.3 | convolution fusion | flops 806878208 | bytes 3215360 | tf_op jit(solution)/shard_map/cond/branch_1_fun/rkgd,nkd->kgrn/dot_general | solution.py:45
  83.0 0.4 fusion.5
  83.5 0.6 copy-done
  84.0 1.1 %reshape.69 = f32[512,2,128]{2,1,0:T(2,128)} reshape(f32[512,256]{1,0:T(8,128)S(1)} %copy-done) | data formatting | bytes 1048576 | tf_op jit(solution)/shard_map/cond/branch_1_fun/reshape | solution.py:44
  85.1 3.6 %fusion.3 = f32[2,4,128,128]{2,3,1,0:T(8,128)} fusion(f32[2,512,128,4]{2,1,3,0:T(8,128)S(1)} %get-tuple-element.59, f32[2,4,128]{2,1,0:T(4,128)S(1)} %broadcast_maximum_fusion, pred[128,512]{0,1:T(8,128)(4,1)S(1)} %iota_compare_fusion, f32[512,2,128,1]{2,1,0,3:T(2,128)} %bitcast.52), kind=kOutput, calls=%fused_computation.6 | convolution fusion | flops 806879232 | bytes 3215360 | tf_op jit(solution)/shard_map/cond | solution.py:64
  88.9 0.7 multiply_reduce_fusion
  89.6 1.3 %multiply_add_fusion = f32[2,4,128,128]{2,3,1,0:T(8,128)S(1)} fusion(f32[2,4,128,128]{2,3,1,0:T(8,128)} %get-tuple-element.49, f32[2,4,128,128]{2,3,1,0:T(8,128)S(1)} %get-tuple-element.61, f32[2,4,128]{2,1,0:T(4,128)S(1)} %get-tuple-element.44, f32[2,4]{1,0:T(2,128)S(1)} %broadcast_subtract_fusion, f32[2,4,128]{2,1,0:T(4,128)S(1)} %bitcast.53, ...), kind=kLoop, calls=%fused_computation.20 | loop fusion | flops 786432 | bytes 1585216 | tf_op jit(solution)/shard_map/add | solution.py:88
  90.9 1.0 %copy.23 = f32[128,1024]{1,0:T(8,128)} copy(f32[128,1024]{0,1:T(8,128)S(1)} %bitcast.47) | data formatting | bytes 1048576 | tf_op jit(solution)/shard_map/reshape | solution.py:89
  (30 shorter events, 0.2 us)
Async XLA Ops:
  6.5 56.6 %copy-start.2 = (f32[128,256]{1,0:T(8,128)S(1)}, f32[128,256]{1,0:T(8,128)}, u32[]{:S(2)}) copy-start(f32[128,256]{1,0:T(8,128)} %param.10) | copy-start | bytes 393220
  6.5 64.6 %copy-start.1 = (f32[128,256]{1,0:T(8,128)S(1)}, f32[128,256]{1,0:T(8,128)}, u32[]{:S(2)}) copy-start(f32[128,256]{1,0:T(8,128)} %param.11) | copy-start | bytes 393220
  6.5 73.9 %copy-start.3 = (f32[128,1024]{1,0:T(8,128)S(1)}, f32[128,1024]{1,0:T(8,128)}, u32[]{:S(2)}) copy-start(f32[128,1024]{1,0:T(8,128)} %param.9) | copy-start | bytes 1572868
  6.5 25.6 %reduce-scatter.2.cloned.1.call-start = ((), (), s32[]{:S(2)}) async-start(), calls=%async_computation.1 | async-start | bytes 163840 | tf_op jit(solution)/shard_map/reduce_scatter | solution.py:72
  63.1 7.7 %collective-permute-start = (f32[64,128]{1,0:T(8,128)S(1)}, f32[64,128]{1,0:T(8,128)S(1)}, u32[]{:S(2)}, u32[]{:S(2)}) collective-permute-start(f32[64,128]{1,0:T(8,128)S(1)} %get-tuple-element.42), channel_id=1, source_target_pairs={{0,1},{1,2},{2,3},{3,0},{4,5},{5,6},{6,7},{7,4},{8,9},{9,10},{10,1... | collective-permute-start | bytes 98312 | tf_op jit(solution)/shard_map/ppermute | solution.py:78
  70.8 8.1 %collective-permute-start.1 = (f32[64,128]{1,0:T(8,128)S(1)}, f32[64,128]{1,0:T(8,128)S(1)}, u32[]{:S(2)}, u32[]{:S(2)}) collective-permute-start(f32[64,128]{1,0:T(8,128)S(1)} %collective-permute-done), channel_id=1, source_target_pairs={{0,1},{1,2},{2,3},{3,0},{4,5},{5,6},{6,7},{7,4},{8,9},{9,10},{10,1... | collective-permute-start | bytes 98312 | tf_op jit(solution)/shard_map/ppermute | solution.py:78
  78.9 9.9 %collective-permute-start.2 = (f32[64,128]{1,0:T(8,128)S(1)}, f32[64,128]{1,0:T(8,128)S(1)}, u32[]{:S(2)}, u32[]{:S(2)}) collective-permute-start(f32[64,128]{1,0:T(8,128)S(1)} %collective-permute-done.1), channel_id=1, source_target_pairs={{0,1},{1,2},{2,3},{3,0},{4,5},{5,6},{6,7},{7,4},{8,9},{9,10},{10,1... | collective-permute-start | bytes 98312 | tf_op jit(solution)/shard_map/ppermute | solution.py:78
  80.7 8.9 %copy-start.4 = (f32[1024]{0:T(1024)S(1)}, f32[1024]{0:T(1024)}, u32[]{:S(2)}) copy-start(f32[1024]{0:T(1024)} %param.13) | copy-start | bytes 12292
  83.0 1.0 %copy-start = (f32[512,256]{1,0:T(8,128)S(1)}, f32[512,256]{1,0:T(8,128)}, u32[]{:S(2)}) copy-start(f32[512,256]{1,0:T(8,128)} %get-tuple-element.38) | copy-start | bytes 1572868 | tf_op jit(solution)/shard_map/cond
Sparse Core Ops, SparseCore 0:
  9.8 22.2 reduce-scatter.1
